TPU v7x, 32 devices: a whole 2x2x4 slice. The times are simulated.
32 devices in a mesh: parts: 2 (over y), seq: 8 (over z, x), head: 2 (over core).
Axes of the slice: x: 2, y: 2, z: 4, core: 2. Of those that a mesh axis runs over, the one named last changes fastest.
Arguments:
- frames: bfloat16 [4096, 1024], P(('parts', 'seq'), 'head'), parts along dimension 0, may hold values from -40 to 40
- w_query: bfloat16 [1024, 1024], P(None, 'head'), may hold values from -0.1875 to 0.1875
- w_key: bfloat16 [1024, 1024], P(None, 'head'), may hold values from -0.1875 to 0.1875
- w_value: bfloat16 [1024, 1024], P(None, 'head'), may hold values from -0.1875 to 0.1875
- down_bank: bfloat16 [8, 1024, 128], P(None, 'seq'), may hold values from -0.1875 to 0.1875
- up_bank: bfloat16 [8, 128, 1024], P(None, 'seq', 'head'), may hold values from -0.75 to 0.75
- bank_row: int32 [8], replicated, may hold values from 0 to 7, each once
- lang_ids: int32 [16], P('parts'), parts along dimension 0, may hold values from 0 to 7, as said below
- seg_ids: int32 [16], P('parts'), parts along dimension 0, may hold values from 0 to 1, as said below
- lookback: int32 [16], P('parts'), parts along dimension 0, may hold values from 0 to 3, as said below
Outputs:
- context: bfloat16 [4096, 1024], P(('parts', 'seq'), 'head'), parts along dimension 0
There are 2 independent parts, one for each index of `parts`. A program takes and returns all parts, laid end to end along the dimension named above; an argument that names none is the same for every part. Nothing has to cross between parts.
Inputs may be any that keep to these rules, and one draw needn't show every extreme that they name: `seg_ids`: blocks of one utterance are consecutive: the number is 0 at the first block and never falls; the largest number is reached at the last block. `lang_ids`: all blocks of one utterance have the same language; the last utterance has language 8 - 1. `bank_row`: each language names a different bank row. `lookback`: the value 3 is reached in every draw.
All inputs are finite; a program needn't handle non-finite values.
Results may differ from a plain program's by a relative error of at most 0.0093.
Values may be sent and summed in bfloat16 or wider, within the bound.
A program may use at most 64 MiB of HBM per device.

v0:
```python
import jax
import jax.numpy as jnp
from jax import lax
from jax.sharding import PartitionSpec as P

HD = 64


NEG_LARGE = -1e30


def from_behind(block, axis, distance):
    devices = range(lax.axis_size(axis))
    route = [(i - distance, i) for i in devices if i - distance in devices]
    return lax.ppermute(block, axis, route)


def block_rules(seg_ids, lookback, position, distance, blocks_dev, block_len):
    query_first = position * blocks_dev
    key_first = (position - distance) * blocks_dev
    counter = jnp.arange(blocks_dev, dtype=jnp.int32)
    query_blocks = query_first + counter
    key_blocks = key_first + counter
    query_seg = lax.dynamic_slice_in_dim(seg_ids, query_first, blocks_dev)
    query_reach = lax.dynamic_slice_in_dim(lookback, query_first, blocks_dev)
    key_seg = lax.dynamic_slice_in_dim(seg_ids, jnp.maximum(key_first, 0), blocks_dev)
    allowed = key_blocks[None, :] >= query_blocks[:, None] - query_reach[:, None]
    allowed = allowed & (key_blocks[None, :] <= query_blocks[:, None])
    allowed = allowed & (key_seg[None, :] == query_seg[:, None]) & (key_blocks[None, :] >= 0)
    frames_dev = blocks_dev * block_len
    expanded = jnp.broadcast_to(
        allowed[:, None, :, None], (blocks_dev, block_len, blocks_dev, block_len)
    )
    return (jnp.any(allowed), expanded.reshape(frames_dev, frames_dev))


def attend(carried, query_heads, pair, allowed):
    run_max, run_sum, run_acc = carried
    frames_dev = query_heads.shape[0]
    heads_dev = query_heads.shape[1]
    key_heads = pair[0].reshape(frames_dev, heads_dev, HD)
    value_heads = pair[1].reshape(frames_dev, heads_dev, HD)
    scores = jnp.einsum(
        "qhe,khe->hqk", query_heads, key_heads, preferred_element_type=jnp.float32
    ) * HD ** (-0.5)
    masked = jnp.where(allowed[None], scores, NEG_LARGE)
    new_max = jnp.maximum(run_max, jnp.max(masked, axis=2))
    factor = jnp.exp(run_max - new_max)
    weights = jnp.where(allowed[None], jnp.exp(masked - new_max[:, :, None]), 0.0)
    new_sum = run_sum * factor + jnp.sum(weights, axis=2)
    update = jnp.einsum(
        "hqk,khe->hqe",
        weights.astype(jnp.bfloat16),
        value_heads,
        preferred_element_type=jnp.float32,
    )
    return (new_max, new_sum, run_acc * factor[:, :, None] + update)


def body(
    frames, w_query, w_key, w_value, down_bank, up_bank, bank_row, lang_ids, seg_ids, lookback
):
    seq_count = lax.axis_size("seq")
    position = lax.axis_index("seq")
    frames_dev = frames.shape[0]
    blocks_dev = lang_ids.shape[0] // seq_count
    block_len = frames_dev // blocks_dev
    model_width = w_query.shape[0]
    columns = w_query.shape[1]
    heads_dev = columns // HD
    rank_two = down_bank.shape[2]
    rank_half = rank_two // 2
    wanted = jnp.transpose(jnp.take(bank_row, lang_ids, axis=0).reshape(seq_count, blocks_dev))
    down_send = jnp.take(down_bank, wanted, axis=0)
    up_send = jnp.take(up_bank, wanted, axis=0)
    down_got, up_got = (
        lax.all_to_all(down_send, "seq", split_axis=1, concat_axis=2, tiled=True),
        lax.all_to_all(up_send, "seq", split_axis=1, concat_axis=2, tiled=True),
    )
    down_mine = down_got.reshape(blocks_dev, model_width, rank_two)
    up_mine = up_got.reshape(blocks_dev, rank_two, columns)
    gathered = lax.all_gather(frames, "head", axis=1, tiled=True)
    queries = jnp.dot(gathered, w_query, preferred_element_type=jnp.float32).astype(jnp.bfloat16)
    block_rows = gathered.reshape(blocks_dev, block_len, model_width)
    lowrank = jnp.einsum(
        "bfd,bdr->bfr", block_rows, down_mine, preferred_element_type=jnp.float32
    ).astype(jnp.bfloat16)
    key_extra = jnp.einsum(
        "bfr,brc->bfc",
        lowrank[:, :, :rank_half],
        up_mine[:, :rank_half],
        preferred_element_type=jnp.float32,
    )
    value_extra = jnp.einsum(
        "bfr,brc->bfc",
        lowrank[:, :, rank_half:],
        up_mine[:, rank_half:],
        preferred_element_type=jnp.float32,
    )
    own_keys = (
        jnp.dot(gathered, w_key, preferred_element_type=jnp.float32)
        + key_extra.reshape(frames_dev, columns)
    ).astype(jnp.bfloat16)
    own_values = (
        jnp.dot(gathered, w_value, preferred_element_type=jnp.float32)
        + value_extra.reshape(frames_dev, columns)
    ).astype(jnp.bfloat16)
    own_pair = jnp.stack([own_keys, own_values])
    query_heads = queries.reshape(frames_dev, heads_dev, HD)
    initial = (
        jnp.full((heads_dev, frames_dev), NEG_LARGE, jnp.float32),
        jnp.zeros((heads_dev, frames_dev), jnp.float32),
        jnp.zeros((heads_dev, frames_dev, HD), jnp.float32),
    )

    def visit_tile(carried, pair, distance):
        nonempty, allowed = block_rules(
            seg_ids, lookback, position, distance, blocks_dev, block_len
        )
        return attend(carried, query_heads, pair, allowed)

    carried = visit_tile(initial, own_pair, 0)
    moving = own_pair
    for distance in range(1, 4):
        moving = from_behind(moving, "seq", 1)
        carried = visit_tile(carried, moving, distance)
    run_max, run_sum, run_acc = carried
    context = (run_acc / run_sum[:, :, None]).astype(jnp.bfloat16)
    return jnp.transpose(context, (1, 0, 2)).reshape(frames_dev, columns)


def solution(mesh):
    in_specs = (
        P(("parts", "seq"), "head"),
        P(None, "head"),
        P(None, "head"),
        P(None, "head"),
        P(None, "seq", None),
        P(None, "seq", "head"),
        P(),
        P("parts"),
        P("parts"),
        P("parts"),
    )
    out_specs = P(("parts", "seq"), "head")
    return jax.shard_map(body, mesh=mesh, in_specs=in_specs, out_specs=out_specs, check_vma=False)
```

profile of v0, /device:TPU:24, one launch (start us, length us, event | category | flops | bytes accessed | tf_op | source)
XLA Modules:
  0.0 89.0 jit_solution(13994182844518407746)
XLA Ops:
  0.0 0.0 copy-start
  0.0 0.0 copy-start.10
  0.0 0.0 copy-start.5
  0.0 0.8 compare_select_fusion.1
  0.8 1.3 %gather_fusion = s32[8]{0:T(128)S(1)} fusion(s32[8]{0:T(128)} %param.16, s32[1024]{0:T(1024)S(1)} %pad_clamp_fusion.1), kind=kCustom, calls=%fused_computation | custom fusion | bytes 96 | tf_op jit(solution)/shard_map/jit(_take)/gather | solution.py:73
  2.1 0.7 compare_and_fusion
  2.8 1.5 %gather_fusion.1 = bf16[8,128,128]{2,1,0:T(8,128)(2,1)S(1)} fusion(bf16[8,128,128]{2,1,0:T(8,128)(2,1)} %param.14, s32[1024]{0:T(1024)S(1)} %pad_clamp_fusion), kind=kCustom, calls=%fused_computation.1 | custom fusion | bytes 524320 | tf_op jit(solution)/shard_map/jit(_take)/gather | solution.py:74
  4.3 0.8 bitcast_select_fusion
  5.1 6.0 %all-to-all-start = ((bf16[1,8,128,128]{3,2,0,1:T(8,128)(2,1)}), bf16[1,8,128,128]{3,2,0,1:T(8,128)(2,1)S(1)}, u32[]{:S(2)}, u32[]{:S(2)}) async-start(bf16[1,8,128,128]{3,2,0,1:T(8,128)(2,1)} %bitcast_select_fusion), calls=%async_computation | async-start | bytes 524288 | tf_op jit(solution)/shard_map/all_to_all | solution.py:77
  11.2 0.0 copy-done.12
  11.2 0.6 dynamic_slice.24
  12.3 0.7 fusion.72
  18.0 0.0 copy-done.10
  18.0 0.6 gather_fusion.2
  18.6 0.7 bitcast_select_fusion.1
  19.3 0.0 all-to-all-done
  19.3 6.0 %all-to-all-start.1 = ((bf16[1,8,16,512]{3,2,0,1:T(8,128)(2,1)}), bf16[1,8,16,512]{3,2,0,1:T(8,128)(2,1)S(1)}, u32[]{:S(2)}, u32[]{:S(2)}) async-start(bf16[1,8,16,512]{3,2,0,1:T(8,128)(2,1)} %bitcast_select_fusion.1), calls=%async_computation.1 | async-start | bytes 262144 | tf_op jit(solution)/shard_map/all_to_all | solution.py:78
  25.3 0.0 copy-done.5
  25.3 2.2 %all_gather.3 = bf16[256,1024]{1,0:T(8,128)(2,1)S(1)} all-gather(bf16[256,512]{1,0:T(8,128)(2,1)S(1)} %copy-done.5), channel_id=1, replica_groups=mesh['parts'=2,'seq'=8,'head'=2] {'head'}, dimensions={1}, use_global_device_ids=true | all-gather | bytes 786432 | tf_op jit(solution)/shard_map/all_gather | solution.py:82
  27.5 0.3 fusion.23
  27.8 1.6 %all-to-all-done.1 = bf16[1,8,16,512]{3,2,0,1:T(8,128)(2,1)S(1)} async-done(((bf16[1,8,16,512]{3,2,0,1:T(8,128)(2,1)}), bf16[1,8,16,512]{3,2,0,1:T(8,128)(2,1)S(1)}, u32[]{:S(2)}, u32[]{:S(2)}) %all-to-all-start.1) | async-done | bytes 131104 | tf_op jit(solution)/shard_map/all_to_all | solution.py:78
  29.4 0.2 fusion.44
  29.6 0.2 fusion.45
  29.9 0.0 copy-done
  29.9 0.4 fusion.21
  30.3 0.0 copy-done.4
  30.3 0.0 copy-start.3
  30.3 0.4 fusion.20
  30.8 0.8 pad_maximum_fusion
  31.6 3.0 %collective-permute-start = (bf16[2,256,512]{2,1,0:T(8,128)(2,1)}, bf16[2,256,512]{2,1,0:T(8,128)(2,1)}, u32[]{:S(2)}, u32[]{:S(2)}) collective-permute-start(bf16[2,256,512]{2,1,0:T(8,128)(2,1)} %pad_maximum_fusion), channel_id=1, source_target_pairs={{0,2},{2,4},{4,6},{6,8},{8,10},{10,12},{12,14},{1,3},{3,5},{5,7},{... | collective-permute-start | bytes 1572872 | tf_op jit(solution)/shard_map/ppermute | solution.py:15
  34.6 0.4 convolution_convert_fusion
  35.1 0.1 copy.42
  35.3 0.8 copy.44
  36.1 0.8 copy.43
  37.0 1.4 %fusion = (f32[8,256]{1,0:T(8,128)S(1)}, f32[8,256,256]{1,2,0:T(8,128)S(1)}) fusion(pred[]{:T(512)} %bitcast.3, bf16[256,8,64]{0,2,1:T(8,128)(2,1)S(1)} %bitcast.158, bf16[256,8,64]{0,2,1:T(8,128)(2,1)} %bitcast.165), kind=kOutput, calls=%fused_computation.11 | convolution fusion | flops 68679680 | bytes 2629633 | tf_op jit(solution)/shard_map/qhe,khe->hqk/dot_general | solution.py:43
  38.4 8.7 %collective-permute-done = bf16[2,256,512]{2,1,0:T(8,128)(2,1)} collective-permute-done((bf16[2,256,512]{2,1,0:T(8,128)(2,1)}, bf16[2,256,512]{2,1,0:T(8,128)(2,1)}, u32[]{:S(2)}, u32[]{:S(2)}) %collective-permute-start) | collective-permute-done | bytes 524320 | tf_op jit(solution)/shard_map/ppermute | solution.py:15
  47.1 2.5 %collective-permute-start.1 = (bf16[2,256,512]{2,1,0:T(8,128)(2,1)}, bf16[2,256,512]{2,1,0:T(8,128)(2,1)}, u32[]{:S(2)}, u32[]{:S(2)}) collective-permute-start(bf16[2,256,512]{2,1,0:T(8,128)(2,1)} %collective-permute-done), channel_id=1, source_target_pairs={{0,2},{2,4},{4,6},{6,8},{8,10},{10,12},{12,14},{1,3},{3,5},{5,7},{... | collective-permute-start | bytes 1572872 | tf_op jit(solution)/shard_map/ppermute | solution.py:15
  49.6 1.9 %fusion.71 = (bf16[1,256,512]{2,1,0:T(8,128)(2,1)}, bf16[1,256,512]{2,1,0:T(8,128)(2,1)}) fusion(bf16[2,256,512]{2,1,0:T(8,128)(2,1)} %collective-permute-done), kind=kLoop, calls=%fused_computation.108 | loop fusion | bytes 1048576 | tf_op jit(solution)/shard_map/slice | solution.py:42
  51.5 1.8 %copy.47 = bf16[1,256,512]{1,2,0:T(8,128)(2,1)} copy(bf16[1,256,512]{2,1,0:T(8,128)(2,1)} %get-tuple-element.17) | data formatting | bytes 524288 | tf_op jit(solution)/shard_map/slice | solution.py:42
  53.3 1.8 %copy.46 = bf16[1,256,512]{1,2,0:T(8,128)(2,1)} copy(bf16[1,256,512]{2,1,0:T(8,128)(2,1)} %get-tuple-element.18) | data formatting | bytes 524288 | tf_op jit(solution)/shard_map/slice | solution.py:41
  55.0 2.8 %fusion.1 = (f32[8,256]{1,0:T(8,128)S(1)}, f32[8,256,256]{1,2,0:T(8,128)}) fusion(pred[]{:T(512)} %bitcast.22, bf16[256,8,64]{0,2,1:T(8,128)(2,1)S(1)} %bitcast.159, bf16[256,8,64]{0,2,1:T(8,128)(2,1)} %bitcast.166), kind=kOutput, calls=%fused_computation.12 | convolution fusion | flops 68679680 | bytes 2629633 | tf_op jit(solution)/shard_map/qhe,khe->hqk/dot_general | solution.py:43
  57.8 3.9 %collective-permute-done.1 = bf16[2,256,512]{2,1,0:T(8,128)(2,1)} collective-permute-done((bf16[2,256,512]{2,1,0:T(8,128)(2,1)}, bf16[2,256,512]{2,1,0:T(8,128)(2,1)}, u32[]{:S(2)}, u32[]{:S(2)}) %collective-permute-start.1) | collective-permute-done | bytes 524320 | tf_op jit(solution)/shard_map/ppermute | solution.py:15
  61.7 1.9 %collective-permute-start.2 = (bf16[2,256,512]{2,1,0:T(8,128)(2,1)}, bf16[2,256,512]{2,1,0:T(8,128)(2,1)}, u32[]{:S(2)}, u32[]{:S(2)}) collective-permute-start(bf16[2,256,512]{2,1,0:T(8,128)(2,1)} %collective-permute-done.1), channel_id=1, source_target_pairs={{0,2},{2,4},{4,6},{6,8},{8,10},{10,12},{12,14},{1,3},{3,5},{5,7},{... | collective-permute-start | bytes 1572872 | tf_op jit(solution)/shard_map/ppermute | solution.py:15
  63.6 1.9 %fusion.70 = (bf16[1,256,512]{2,1,0:T(8,128)(2,1)}, bf16[1,256,512]{2,1,0:T(8,128)(2,1)}) fusion(bf16[2,256,512]{2,1,0:T(8,128)(2,1)} %collective-permute-done.1), kind=kLoop, calls=%fused_computation.107 | loop fusion | bytes 1048576 | tf_op jit(solution)/shard_map/slice | solution.py:42
  65.5 1.8 %copy.50 = bf16[1,256,512]{1,2,0:T(8,128)(2,1)} copy(bf16[1,256,512]{2,1,0:T(8,128)(2,1)} %get-tuple-element.15) | data formatting | bytes 524288 | tf_op jit(solution)/shard_map/slice | solution.py:42
  67.3 1.8 %copy.49 = bf16[1,256,512]{1,2,0:T(8,128)(2,1)} copy(bf16[1,256,512]{2,1,0:T(8,128)(2,1)} %get-tuple-element.16) | data formatting | bytes 524288 | tf_op jit(solution)/shard_map/slice | solution.py:41
  69.1 2.8 %fusion.2 = (f32[8,256]{1,0:T(8,128)S(1)}, f32[8,256,256]{1,2,0:T(8,128)}) fusion(pred[]{:T(512)} %bitcast.31, bf16[256,8,64]{0,2,1:T(8,128)(2,1)S(1)} %bitcast.160, bf16[256,8,64]{0,2,1:T(8,128)(2,1)} %bitcast.167), kind=kOutput, calls=%fused_computation.13 | convolution fusion | flops 68679680 | bytes 2629633 | tf_op jit(solution)/shard_map/qhe,khe->hqk/dot_general | solution.py:43
  71.8 3.5 %collective-permute-done.2 = bf16[2,256,512]{2,1,0:T(8,128)(2,1)} collective-permute-done((bf16[2,256,512]{2,1,0:T(8,128)(2,1)}, bf16[2,256,512]{2,1,0:T(8,128)(2,1)}, u32[]{:S(2)}, u32[]{:S(2)}) %collective-permute-start.2) | collective-permute-done | bytes 524320 | tf_op jit(solution)/shard_map/ppermute | solution.py:15
  75.3 1.9 %fusion.69 = (bf16[1,256,512]{2,1,0:T(8,128)(2,1)}, bf16[1,256,512]{2,1,0:T(8,128)(2,1)}) fusion(bf16[2,256,512]{2,1,0:T(8,128)(2,1)} %collective-permute-done.2), kind=kLoop, calls=%fused_computation.106 | loop fusion | bytes 1048576 | tf_op jit(solution)/shard_map/slice | solution.py:42
  77.2 1.8 %copy.53 = bf16[1,256,512]{1,2,0:T(8,128)(2,1)} copy(bf16[1,256,512]{2,1,0:T(8,128)(2,1)} %get-tuple-element.13) | data formatting | bytes 524288 | tf_op jit(solution)/shard_map/slice | solution.py:42
  79.0 1.8 %copy.52 = bf16[1,256,512]{1,2,0:T(8,128)(2,1)} copy(bf16[1,256,512]{2,1,0:T(8,128)(2,1)} %get-tuple-element.14) | data formatting | bytes 524288 | tf_op jit(solution)/shard_map/slice | solution.py:41
  80.8 1.6 %fusion.3 = (f32[8,256]{1,0:T(8,128)S(1)}, f32[8,256,256]{1,2,0:T(8,128)S(1)}) fusion(pred[]{:T(512)} %bitcast.38, bf16[256,8,64]{0,2,1:T(8,128)(2,1)S(1)} %bitcast.161, bf16[256,8,64]{0,2,1:T(8,128)(2,1)} %bitcast.164), kind=kOutput, calls=%fused_computation.14 | convolution fusion | flops 68679680 | bytes 2629633 | tf_op jit(solution)/shard_map/qhe,khe->hqk/dot_general | solution.py:43
  82.4 0.1 copy-done.2
  82.4 1.0 %fusion.8 = (f32[8,256]{1,0:T(8,128)S(1)}, f32[8,256]{1,0:T(8,128)S(1)}) fusion(f32[8,256,256]{1,2,0:T(8,128)S(1)} %copy-done.2, f32[8,256]{1,0:T(8,128)S(1)} %get-tuple-element.9, pred[]{:T(512)} %bitcast.31, f32[8,256]{1,0:T(8,128)S(1)} %get-tuple-element.8, f32[8,256,256]{1,2,0:T(8,128)S(1)} %get-tuple-element.28, pred[]{:T(512)} %bitcast.38), kind=kLoop, calls=%fused_computation.19 | loop fusion | flops 5238784 | bytes 4227074 | tf_op jit(solution)/shard_map/reduce_sum | solution.py:50
  83.4 0.6 copy-done.1
  84.0 1.0 %fusion.4 = (f32[8,256]{1,0:T(8,128)S(1)}, f32[8,256]{1,0:T(8,128)S(1)}) fusion(f32[8,256,256]{1,2,0:T(8,128)S(1)} %get-tuple-element.34, f32[8,256]{1,0:T(8,128)S(1)} %get-tuple-element.21, pred[]{:T(512)} %bitcast.3, f32[8,256]{1,0:T(8,128)S(1)} %get-tuple-element.10, f32[8,256,256]{1,2,0:T(8,128)S(1)} %copy-done.1, pred[]{:T(512)} %bitcast.22), kind=kLoop, calls=%fused_computation.15 | loop fusion | flops 5238784 | bytes 4227074 | tf_op jit(solution)/shard_map/reduce_sum | solution.py:50
  85.1 0.6 fusion.19
  85.7 0.4 copy-done.7
  86.0 0.6 fusion.17
  86.6 0.0 copy-done.8
  86.6 0.6 fusion.15
  87.2 0.4 copy-done.9
  87.5 0.6 fusion.22
  88.1 0.8 copy.55
  (16 shorter events, 0.1 us)
Async XLA Ops:
  0.0 29.9 %copy-start = (bf16[1024,512]{1,0:T(8,128)(2,1)S(1)}, bf16[1024,512]{1,0:T(8,128)(2,1)}, u32[]{:S(2)}) copy-start(bf16[1024,512]{1,0:T(8,128)(2,1)} %param.13) | copy-start | bytes 3145732
  0.0 11.2 %copy-start.12 = (s32[8]{0:T(128)S(1)}, s32[8]{0:T(128)}, u32[]{:S(2)}) copy-start(s32[8]{0:T(128)} %param.19) | copy-start | bytes 100
  0.0 12.3 %copy-start.11 = (s32[8]{0:T(128)S(1)}, s32[8]{0:T(128)}, u32[]{:S(2)}) copy-start(s32[8]{0:T(128)} %param.18) | copy-start | bytes 100
  0.0 18.0 %copy-start.10 = (bf16[8,16,512]{2,1,0:T(8,128)(2,1)S(1)}, bf16[8,16,512]{2,1,0:T(8,128)(2,1)}, u32[]{:S(2)}) copy-start(bf16[8,16,512]{2,1,0:T(8,128)(2,1)} %param.15) | copy-start | bytes 393220
  0.0 25.3 %copy-start.5 = (bf16[256,512]{1,0:T(8,128)(2,1)S(1)}, bf16[256,512]{1,0:T(8,128)(2,1)}, u32[]{:S(2)}) copy-start(bf16[256,512]{1,0:T(8,128)(2,1)} %param.10) | copy-start | bytes 786436
  5.1 14.2 %all-to-all-start = ((bf16[1,8,128,128]{3,2,0,1:T(8,128)(2,1)}), bf16[1,8,128,128]{3,2,0,1:T(8,128)(2,1)S(1)}, u32[]{:S(2)}, u32[]{:S(2)}) async-start(bf16[1,8,128,128]{3,2,0,1:T(8,128)(2,1)} %bitcast_select_fusion), calls=%async_computation | async-start | bytes 524288 | tf_op jit(solution)/shard_map/all_to_all | solution.py:77
  19.3 10.1 %all-to-all-start.1 = ((bf16[1,8,16,512]{3,2,0,1:T(8,128)(2,1)}), bf16[1,8,16,512]{3,2,0,1:T(8,128)(2,1)S(1)}, u32[]{:S(2)}, u32[]{:S(2)}) async-start(bf16[1,8,16,512]{3,2,0,1:T(8,128)(2,1)} %bitcast_select_fusion.1), calls=%async_computation.1 | async-start | bytes 262144 | tf_op jit(solution)/shard_map/all_to_all | solution.py:78
  27.5 2.9 %copy-start.4 = (bf16[1024,512]{1,0:T(8,128)(2,1)S(1)}, bf16[1024,512]{1,0:T(8,128)(2,1)}, u32[]{:S(2)}) copy-start(bf16[1024,512]{1,0:T(8,128)(2,1)} %param.12) | copy-start | bytes 3145732
  30.3 4.3 %copy-start.3 = (bf16[1024,512]{1,0:T(8,128)(2,1)S(1)}, bf16[1024,512]{1,0:T(8,128)(2,1)}, u32[]{:S(2)}) copy-start(bf16[1024,512]{1,0:T(8,128)(2,1)} %param.11) | copy-start | bytes 3145732
  31.6 15.5 %collective-permute-start = (bf16[2,256,512]{2,1,0:T(8,128)(2,1)}, bf16[2,256,512]{2,1,0:T(8,128)(2,1)}, u32[]{:S(2)}, u32[]{:S(2)}) collective-permute-start(bf16[2,256,512]{2,1,0:T(8,128)(2,1)} %pad_maximum_fusion), channel_id=1, source_target_pairs={{0,2},{2,4},{4,6},{6,8},{8,10},{10,12},{12,14},{1,3},{3,5},{5,7},{... | collective-permute-start | bytes 1572872 | tf_op jit(solution)/shard_map/ppermute | solution.py:15
  47.1 14.6 %collective-permute-start.1 = (bf16[2,256,512]{2,1,0:T(8,128)(2,1)}, bf16[2,256,512]{2,1,0:T(8,128)(2,1)}, u32[]{:S(2)}, u32[]{:S(2)}) collective-permute-start(bf16[2,256,512]{2,1,0:T(8,128)(2,1)} %collective-permute-done), channel_id=1, source_target_pairs={{0,2},{2,4},{4,6},{6,8},{8,10},{10,12},{12,14},{1,3},{3,5},{5,7},{... | collective-permute-start | bytes 1572872 | tf_op jit(solution)/shard_map/ppermute | solution.py:15
  61.7 13.6 %collective-permute-start.2 = (bf16[2,256,512]{2,1,0:T(8,128)(2,1)}, bf16[2,256,512]{2,1,0:T(8,128)(2,1)}, u32[]{:S(2)}, u32[]{:S(2)}) collective-permute-start(bf16[2,256,512]{2,1,0:T(8,128)(2,1)} %collective-permute-done.1), channel_id=1, source_target_pairs={{0,2},{2,4},{4,6},{6,8},{8,10},{10,12},{12,14},{1,3},{3,5},{5,7},{... | collective-permute-start | bytes 1572872 | tf_op jit(solution)/shard_map/ppermute | solution.py:15
  80.8 1.7 %copy-start.2 = (f32[8,256,256]{1,2,0:T(8,128)S(1)}, f32[8,256,256]{1,2,0:T(8,128)}, u32[]{:S(2)}) copy-start(f32[8,256,256]{1,2,0:T(8,128)} %get-tuple-element.30) | copy-start | bytes 6291460
  82.4 1.6 %copy-start.1 = (f32[8,256,256]{1,2,0:T(8,128)S(1)}, f32[8,256,256]{1,2,0:T(8,128)}, u32[]{:S(2)}) copy-start(f32[8,256,256]{1,2,0:T(8,128)} %get-tuple-element.32) | copy-start | bytes 6291460
  84.0 1.1 %copy-start.6 = (bf16[256,512]{0,1:T(8,128)(2,1)S(1)}, bf16[256,512]{0,1:T(8,128)(2,1)}, u32[]{:S(2)}) copy-start(bf16[256,512]{0,1:T(8,128)(2,1)} %copy.44) | copy-start | bytes 786436
  85.1 1.0 %copy-start.7 = (bf16[1,256,512]{1,2,0:T(8,128)(2,1)S(1)}, bf16[1,256,512]{1,2,0:T(8,128)(2,1)}, u32[]{:S(2)}) copy-start(bf16[1,256,512]{1,2,0:T(8,128)(2,1)} %copy.47) | copy-start | bytes 786436
  85.7 1.0 %copy-start.8 = (bf16[1,256,512]{1,2,0:T(8,128)(2,1)S(1)}, bf16[1,256,512]{1,2,0:T(8,128)(2,1)}, u32[]{:S(2)}) copy-start(bf16[1,256,512]{1,2,0:T(8,128)(2,1)} %copy.50) | copy-start | bytes 786436
  86.6 1.0 %copy-start.9 = (bf16[1,256,512]{1,2,0:T(8,128)(2,1)S(1)}, bf16[1,256,512]{1,2,0:T(8,128)(2,1)}, u32[]{:S(2)}) copy-start(bf16[1,256,512]{1,2,0:T(8,128)(2,1)} %copy.53) | copy-start | bytes 786436
where the time goes:
time: 89.9 us; the launch traced here: 89 us
  local copies, waits for them, and re-layouts  25.1 us (28%)
  starting transfers between devices  19.4 us (22%)
  waiting for transfers between devices  17.7 us (20%)
  matrix products  12.9 us (14%)
  between operations  5.86 us (7%)
  other arithmetic  5.85 us (7%)
  blocking collectives  2.17 us (2%)
    ppermute x3, waiting for transfers between devices, from_behind(): return lax.ppermute(block, axis, route)  16.1 us
    slice x6, local copies, waits for them, and re-layouts, attend(): value_heads = pair[1].reshape(frames_dev, heads_dev, HD)  11 us
    dot_general x4, matrix products, attend(): jnp.einsum('qhe,khe->hqk', query_heads, key_heads, preferred_element_type...  8.55 us
    ppermute x3, starting transfers between devices, from_behind(): return lax.ppermute(block, axis, route)  7.39 us
    all_to_all x1, starting transfers between devices, body(): lax.all_to_all(down_send, 'seq', split_axis=1, concat_axis=2, tiled=True)  6.03 us
    all_to_all x1, starting transfers between devices, body(): lax.all_to_all(up_send, 'seq', split_axis=1, concat_axis=2, tiled=True)  6 us
    slice x3, local copies, waits for them, and re-layouts, attend(): key_heads = pair[0].reshape(frames_dev, heads_dev, HD)  5.36 us
    dot_general x4, matrix products, attend(): jnp.einsum('hqk,khe->hqe', weights.astype(jnp.bfloat16), value_heads, pre...  2.27 us
  transfers between devices with their start and end apart: 5, of which 4 were waited for; matrix products, arithmetic and copies ran while one was open for 26% of the time, Pallas kernels for 0%

commit v1 on v0

v1 whole, which is shorter than its diff:
```python
import functools

import jax
import jax.numpy as jnp
from jax import lax
from jax.experimental import pallas as pl
from jax.experimental.pallas import tpu as pltpu
from jax.sharding import PartitionSpec as P

HD = 64
LOOK = 3
NEG_LARGE = -1e30
MESH = pl.DeviceIdType.MESH


def dot(a, b):
    return jnp.dot(a, b, preferred_element_type=jnp.float32)


def dot_t(a, b):
    return lax.dot_general(a, b, (((1,), (1,)), ((), ())), preferred_element_type=jnp.float32)


def kernel(
    n, inside,
    bank_row, lang_ids, seg_ids, lookback, frames, w_query, w_key, w_value, down, up,
    out,
    x, wq, wk, wv, d_mine, u_mine, d_bank, u_bank, d_send, u_send, q_two, acc, top, tot,
    local_sem, f_send, f_recv, t_send, t_recv, a_send, a_recv, dt_send, dt_recv,
):
    me = lax.axis_index("seq")
    h = lax.axis_index("head")
    rows, half = frames.shape
    columns = w_query.shape[1]
    pairs = columns // 128

    def local(src, dst, i):
        return pltpu.make_async_copy(src, dst, local_sem.at[i])

    own = local(frames, x.at[0, h], 0)
    own.start()
    if inside:
        bank_d = local(down, d_bank, 4)
        bank_u = local(up, u_bank, 5)
    else:
        bank_d = local(down, d_mine, 4)
        bank_u = local(up, u_mine, 5)
    bank_d.start()
    bank_u.start()
    weights = [local(w_query, wq, 1), local(w_key, wk, 2), local(w_value, wv, 3)]
    for c in weights:
        c.start()

    barrier = pltpu.get_barrier_semaphore()
    twin = {"head": 1 - h}
    if inside:
        steps = list(range(1, n))
    else:
        steps = [1, 2, 3, n - 3, n - 2, n - 1]
    pl.semaphore_signal(barrier, inc=1, device_id=twin, device_id_type=MESH)
    for k in steps:
        pl.semaphore_signal(barrier, inc=1, device_id={"seq": lax.rem(me + k, n)}, device_id_type=MESH)
    pl.semaphore_wait(barrier, len(steps) + 1)

    def frame_copy(d):
        return pltpu.make_async_remote_copy(
            src_ref=frames, dst_ref=x.at[d, h], send_sem=f_send.at[d - 1], recv_sem=f_recv.at[d - 1],
            device_id={"seq": lax.rem(me + d, n)}, device_id_type=MESH)

    def twin_copy(d):
        return pltpu.make_async_remote_copy(
            src_ref=frames if d == 0 else x.at[d, h], dst_ref=x.at[d, h],
            send_sem=t_send.at[d], recv_sem=t_recv.at[d], device_id=twin, device_id_type=MESH)

    twin_copy(0).start()

    def adapter_copies(k):
        to = {"seq": lax.rem(me + k, n)}
        return (
            pltpu.make_async_remote_copy(
                src_ref=d_send.at[k - 1], dst_ref=d_mine.at[me, h], send_sem=a_send.at[0, k - 1],
                recv_sem=a_recv.at[0, k - 1], device_id=to, device_id_type=MESH),
            pltpu.make_async_remote_copy(
                src_ref=u_send.at[k - 1], dst_ref=u_mine.at[me], send_sem=a_send.at[1, k - 1],
                recv_sem=a_recv.at[1, k - 1], device_id=to, device_id_type=MESH))

    def adapter_arrivals(k):
        source = lax.rem(me + n - k, n)
        return (
            pltpu.make_async_remote_copy(
                src_ref=d_send.at[k - 1], dst_ref=d_mine.at[source, h], send_sem=a_send.at[0, k - 1],
                recv_sem=a_recv.at[0, k - 1], device_id=twin, device_id_type=MESH),
            pltpu.make_async_remote_copy(
                src_ref=u_send.at[k - 1], dst_ref=u_mine.at[source], send_sem=a_send.at[1, k - 1],
                recv_sem=a_recv.at[1, k - 1], device_id=twin, device_id_type=MESH))

    if inside:
        piece = d_send.shape[1]
        first = pl.multiple_of(h * piece, piece)
        bank_d.wait()
        bank_u.wait()
        for k in range(1, n):
            row = bank_row[lang_ids[lax.rem(me + k, n)]]
            d_send[k - 1] = d_bank[row, pl.ds(first, piece), :]
            u_send[k - 1] = u_bank[row]
            for c in adapter_copies(k):
                c.start()
        row = bank_row[lang_ids[me]]
        d_mine[me, h] = d_bank[row, pl.ds(first, piece), :]
        u_mine[me] = u_bank[row]

    for d in range(1, LOOK + 1):
        @pl.when(me + d < n)
        def _():
            frame_copy(d).start()

    lane = lax.broadcasted_iota(jnp.int32, (rows, 128), 1)
    low = lane < HD

    own.wait()
    twin_copy(0).wait_recv()
    for c in weights:
        c.wait()

    def project(d, w):
        return dot(x[d, 0], w[:half]) + dot(x[d, 1], w[half:])

    q = (project(0, wq).astype(jnp.bfloat16).astype(jnp.float32) * HD ** (-0.5)).astype(jnp.bfloat16)
    for j in range(pairs):
        part = q[:, j * 128:(j + 1) * 128]
        q_two[0, :, j * 128:(j + 1) * 128] = jnp.where(low, part, jnp.zeros_like(part))
        q_two[1, :, j * 128:(j + 1) * 128] = jnp.where(low, jnp.zeros_like(part), part)

    if inside:
        for k in range(1, n):
            for c in adapter_arrivals(k):
                c.wait_recv()
        d_hand = pltpu.make_async_remote_copy(
            src_ref=d_mine.at[:, h], dst_ref=d_mine.at[:, h], send_sem=dt_send, recv_sem=dt_recv,
            device_id=twin, device_id_type=MESH)
        d_hand.start()
        d_hand.wait_recv()
    else:
        bank_d.wait()
        bank_u.wait()

    def hand_over(d):
        @pl.when(me >= d)
        def _():
            frame_copy(d).wait_recv()
            twin_copy(d).start()

        @pl.when(me < d)
        def _():
            x[d] = jnp.zeros(x.shape[1:], x.dtype)

    def arrived(d):
        @pl.when(me >= d)
        def _():
            twin_copy(d).wait_recv()

    def keys_values(d):
        flat_d = d_mine[...].reshape(2 * half, 128)
        flat_u = u_mine[...].reshape(128, columns)
        low_rank = (dot(x[d, 0], flat_d[:half]) + dot(x[d, 1], flat_d[half:])).astype(jnp.bfloat16)
        none = jnp.zeros_like(low_rank)
        key = (project(d, wk) + dot(jnp.where(low, low_rank, none), flat_u)).astype(jnp.bfloat16)
        value = (project(d, wv) + dot(jnp.where(low, none, low_rank), flat_u)).astype(jnp.bfloat16)
        return key, value

    def attend(d):
        key, value = keys_values(d)
        if d > 0:
            behind = jnp.maximum(me - d, 0)
            allowed = (me >= d) & (lookback[me] >= d) & (seg_ids[behind] == seg_ids[me])
            bias = jnp.where(allowed, 0.0, NEG_LARGE).astype(jnp.float32)
        for j in range(pairs):
            cols = slice(j * 128, (j + 1) * 128)
            outs, factors = [], []
            for e in range(2):
                head = 2 * j + e
                s = dot_t(q_two[e, :, cols], key[:, cols])
                if d == 0:
                    m = jnp.max(s, axis=1, keepdims=True)
                    w = jnp.exp(s - m)
                    total = jnp.sum(w, axis=1, keepdims=True)
                else:
                    s = s + bias
                    before = top[head][:, :1]
                    m = jnp.maximum(before, jnp.max(s, axis=1, keepdims=True))
                    w = jnp.exp(s - m)
                    factor = jnp.exp(before - m)
                    total = tot[head][:, :1] * factor + jnp.sum(w, axis=1, keepdims=True)
                    factors.append(factor)
                top[head] = jnp.broadcast_to(m, (rows, 128))
                tot[head] = jnp.broadcast_to(total, (rows, 128))
                outs.append(dot(w.astype(jnp.bfloat16), value[:, cols]))
            new = jnp.where(low, outs[0], outs[1])
            if d > 0:
                new = new + acc[:, cols] * jnp.where(low, factors[0], factors[1])
            if d == LOOK:
                new = new / jnp.where(low, tot[2 * j], tot[2 * j + 1])
                out[:, cols] = new.astype(out.dtype)
            else:
                acc[:, cols] = new

    attend(0)
    for d in range(1, LOOK + 1):
        hand_over(d)
        arrived(d)
        attend(d)

    for d in range(LOOK + 1):
        if d == 0:
            twin_copy(0).wait_send()
        else:
            @pl.when(me >= d)
            def _():
                twin_copy(d).wait_send()

            @pl.when(me + d < n)
            def _():
                frame_copy(d).wait_send()
    if inside:
        for k in range(1, n):
            for c in adapter_copies(k):
                c.wait_send()
        d_hand.wait_send()


def body(frames, w_query, w_key, w_value, down_bank, up_bank, bank_row, lang_ids, seg_ids, lookback):
    n = lax.axis_size("seq")
    rows, half = frames.shape
    columns = w_query.shape[1]
    bank_rows, d_rows, rank_two = down_bank.shape
    u_rows = up_bank.shape[1]
    inside = d_rows % 32 == 0 and u_rows % 16 == 0
    bf16, f32 = jnp.bfloat16, jnp.float32
    if inside:
        down, up = down_bank, up_bank
        d_shape, u_shape = (n, 2, d_rows // 2, rank_two), (n, u_rows, columns)
        banks = [down_bank.shape, up_bank.shape, (n - 1, d_rows // 2, rank_two), (n - 1, u_rows, columns)]
    else:
        wanted = jnp.take(bank_row, lang_ids, axis=0)
        down = lax.all_to_all(jnp.take(down_bank, wanted, axis=0), "seq", split_axis=0, concat_axis=1, tiled=True)
        up = lax.all_to_all(jnp.take(up_bank, wanted, axis=0), "seq", split_axis=0, concat_axis=1, tiled=True)
        down, up = down.reshape(d_rows * n, rank_two), up.reshape(u_rows * n, columns)
        d_shape, u_shape = down.shape, up.shape
        banks = [(16, 128)] * 4
    steps = n - 1 if inside else 1
    smem = pl.BlockSpec(memory_space=pltpu.SMEM)
    anywhere = pl.BlockSpec(memory_space=pl.ANY)
    dma = pltpu.SemaphoreType.DMA
    return pl.pallas_call(
        functools.partial(kernel, n, inside),
        out_shape=jax.ShapeDtypeStruct((rows, columns), bf16),
        in_specs=[smem] * 4 + [anywhere] * 6,
        out_specs=pl.BlockSpec(memory_space=pltpu.VMEM),
        scratch_shapes=[
            pltpu.VMEM((LOOK + 1, 2, rows, half), bf16),
            *[pltpu.VMEM(w_query.shape, bf16)] * 3,
            pltpu.VMEM(d_shape, bf16),
            pltpu.VMEM(u_shape, bf16),
            *[pltpu.VMEM(s, bf16) for s in banks],
            pltpu.VMEM((2, rows, columns), bf16),
            pltpu.VMEM((rows, columns), f32),
            *[pltpu.VMEM((columns // HD, rows, 128), f32)] * 2,
            dma((6,)), dma((LOOK,)), dma((LOOK,)), dma((LOOK + 1,)), dma((LOOK + 1,)),
            dma((2, steps)), dma((2, steps)), dma, dma,
        ],
        compiler_params=pltpu.CompilerParams(
            collective_id=0, has_side_effects=True, vmem_limit_bytes=50 * 2 ** 20),
        cost_estimate=pl.CostEstimate(flops=6 * 10 ** 9, bytes_accessed=8 * 2 ** 20, transcendentals=2 ** 21),
    )(bank_row, lang_ids, seg_ids, lookback, frames, w_query, w_key, w_value, down, up)


def solution(mesh):
    in_specs = (
        P(("parts", "seq"), "head"),
        P(None, "head"),
        P(None, "head"),
        P(None, "head"),
        P(None, "seq", None),
        P(None, "seq", "head"),
        P(),
        P("parts"),
        P("parts"),
        P("parts"),
    )
    out_specs = P(("parts", "seq"), "head")
    return jax.shard_map(body, mesh=mesh, in_specs=in_specs, out_specs=out_specs, check_vma=False)
```

time: 89.9 us -> 53.6 us (0.60)
  the two profiles are of different devices: /device:TPU:24 before, /device:TPU:18 now
where the time goes in v1:
time: 53.6 us; the launch traced here: 53.3 us
  Pallas kernels  43.5 us (81%)
  local copies, waits for them, and re-layouts  9.8 us (18%)
    pallas_call x1, Pallas kernels, body(): pl.pallas_call(functools.partial(kernel, n, inside), out_shape=jax.ShapeD...  43.5 us
    unnamed x21, local copies, waits for them, and re-layouts  9.8 us

profile of v1, /device:TPU:18, one launch (start us, length us, event | category | flops | bytes accessed | tf_op | source)
XLA Modules:
  0.0 53.3 jit_solution(13556526877217817634)
XLA Ops:
  0.0 0.0 copy-start
  0.0 1.2 %copy-done = bf16[1024,512]{1,0:T(8,128)(2,1)S(1)} copy-done((bf16[1024,512]{1,0:T(8,128)(2,1)S(1)}, bf16[1024,512]{1,0:T(8,128)(2,1)}, u32[]{:S(2)}) %copy-start) | copy-done | bytes 1048600
  1.2 0.0 copy-start.1
  1.2 1.2 %copy-done.1 = bf16[1024,512]{1,0:T(8,128)(2,1)S(1)} copy-done((bf16[1024,512]{1,0:T(8,128)(2,1)S(1)}, bf16[1024,512]{1,0:T(8,128)(2,1)}, u32[]{:S(2)}) %copy-start.1) | copy-done | bytes 1048600
  2.5 0.0 copy-start.2
  2.5 1.2 %copy-done.2 = bf16[1024,512]{1,0:T(8,128)(2,1)S(1)} copy-done((bf16[1024,512]{1,0:T(8,128)(2,1)S(1)}, bf16[1024,512]{1,0:T(8,128)(2,1)}, u32[]{:S(2)}) %copy-start.2) | copy-done | bytes 1048600
  3.7 0.0 copy-start.3
  3.7 0.9 %copy-done.3 = bf16[256,512]{1,0:T(8,128)(2,1)S(1)} copy-done((bf16[256,512]{1,0:T(8,128)(2,1)S(1)}, bf16[256,512]{1,0:T(8,128)(2,1)}, u32[]{:S(2)}) %copy-start.3) | copy-done | bytes 262168
  4.6 0.0 copy-start.4
  4.6 0.9 %copy-done.4 = bf16[8,128,128]{2,1,0:T(8,128)(2,1)S(1)} copy-done((bf16[8,128,128]{2,1,0:T(8,128)(2,1)S(1)}, bf16[8,128,128]{2,1,0:T(8,128)(2,1)}, u32[]{:S(2)}) %copy-start.4) | copy-done | bytes 262168
  5.6 0.0 copy-start.5
  5.6 0.9 %copy-done.5 = bf16[8,16,512]{2,1,0:T(8,128)(2,1)S(1)} copy-done((bf16[8,16,512]{2,1,0:T(8,128)(2,1)S(1)}, bf16[8,16,512]{2,1,0:T(8,128)(2,1)}, u32[]{:S(2)}) %copy-start.5) | copy-done | bytes 131096
  6.5 0.0 copy-start.6
  6.5 0.7 %copy-done.6 = s32[8]{0:T(128)S(1)} copy-done((s32[8]{0:T(128)S(1)}, s32[8]{0:T(128)}, u32[]{:S(2)}) %copy-start.6) | copy-done | bytes 56
  7.1 0.0 copy-start.7
  7.1 0.7 %copy-done.7 = s32[8]{0:T(128)S(1)} copy-done((s32[8]{0:T(128)S(1)}, s32[8]{0:T(128)}, u32[]{:S(2)}) %copy-start.7) | copy-done | bytes 56
  7.8 0.0 copy-start.8
  7.8 0.7 %copy-done.8 = s32[8]{0:T(128)S(1)} copy-done((s32[8]{0:T(128)S(1)}, s32[8]{0:T(128)}, u32[]{:S(2)}) %copy-start.8) | copy-done | bytes 56
  8.4 0.0 copy-start.9
  8.5 0.7 %copy-done.9 = s32[8]{0:T(128)S(1)} copy-done((s32[8]{0:T(128)S(1)}, s32[8]{0:T(128)}, u32[]{:S(2)}) %copy-start.9) | copy-done | bytes 56
  9.1 43.5 %shard_map.100 = bf16[256,512]{1,0:T(8,128)(2,1)S(1)} custom-call(s32[8]{0:T(128)S(1)} %copy-done.6, s32[8]{0:T(128)S(1)} %copy-done.7, s32[8]{0:T(128)S(1)} %copy-done.8, s32[8]{0:T(128)S(1)} %copy-done.9, bf16[256,512]{1,0:T(8,128)(2,1)S(1)} %copy-done.3, bf16[1024,512]{1,0:T(8,128)(2,1)S(1)} %copy-done, bf16[1024,512]{1,0:T(8,128)(2,1)S(1)} %copy-done.1, ...), custom_call_target="tpu_custom_call" | custom-call | flops 6000000000 | bytes 8388608 | tf_op jit(solution)/shard_map/pallas_call | solution.py:254
  52.6 0.7 %copy.12 = bf16[256,512]{1,0:T(8,128)(2,1)} copy(bf16[256,512]{1,0:T(8,128)(2,1)S(1)} %shard_map.100) | data formatting | bytes 524288
Async XLA Ops:
  0.0 1.2 %copy-start = (bf16[1024,512]{1,0:T(8,128)(2,1)S(1)}, bf16[1024,512]{1,0:T(8,128)(2,1)}, u32[]{:S(2)}) copy-start(bf16[1024,512]{1,0:T(8,128)(2,1)} %w_query.1) | copy-start | bytes 3145732
  1.2 1.2 %copy-start.1 = (bf16[1024,512]{1,0:T(8,128)(2,1)S(1)}, bf16[1024,512]{1,0:T(8,128)(2,1)}, u32[]{:S(2)}) copy-start(bf16[1024,512]{1,0:T(8,128)(2,1)} %w_key.1) | copy-start | bytes 3145732
  2.5 1.2 %copy-start.2 = (bf16[1024,512]{1,0:T(8,128)(2,1)S(1)}, bf16[1024,512]{1,0:T(8,128)(2,1)}, u32[]{:S(2)}) copy-start(bf16[1024,512]{1,0:T(8,128)(2,1)} %w_value.1) | copy-start | bytes 3145732
  3.7 0.9 %copy-start.3 = (bf16[256,512]{1,0:T(8,128)(2,1)S(1)}, bf16[256,512]{1,0:T(8,128)(2,1)}, u32[]{:S(2)}) copy-start(bf16[256,512]{1,0:T(8,128)(2,1)} %frames.1) | copy-start | bytes 786436
  4.6 0.9 %copy-start.4 = (bf16[8,128,128]{2,1,0:T(8,128)(2,1)S(1)}, bf16[8,128,128]{2,1,0:T(8,128)(2,1)}, u32[]{:S(2)}) copy-start(bf16[8,128,128]{2,1,0:T(8,128)(2,1)} %down.1) | copy-start | bytes 786436
  5.6 0.9 %copy-start.5 = (bf16[8,16,512]{2,1,0:T(8,128)(2,1)S(1)}, bf16[8,16,512]{2,1,0:T(8,128)(2,1)}, u32[]{:S(2)}) copy-start(bf16[8,16,512]{2,1,0:T(8,128)(2,1)} %up.1) | copy-start | bytes 393220
  6.5 0.7 %copy-start.6 = (s32[8]{0:T(128)S(1)}, s32[8]{0:T(128)}, u32[]{:S(2)}) copy-start(s32[8]{0:T(128)} %bank_row.1) | copy-start | bytes 100
  7.1 0.7 %copy-start.7 = (s32[8]{0:T(128)S(1)}, s32[8]{0:T(128)}, u32[]{:S(2)}) copy-start(s32[8]{0:T(128)} %lang_ids.1) | copy-start | bytes 100
  7.8 0.7 %copy-start.8 = (s32[8]{0:T(128)S(1)}, s32[8]{0:T(128)}, u32[]{:S(2)}) copy-start(s32[8]{0:T(128)} %seg_ids.1) | copy-start | bytes 100
  8.4 0.7 %copy-start.9 = (s32[8]{0:T(128)S(1)}, s32[8]{0:T(128)}, u32[]{:S(2)}) copy-start(s32[8]{0:T(128)} %lookback.1) | copy-start | bytes 100

commit v2 on v1

--- a/solution.py
+++ b/solution.py
@@ -22,9 +22,10 @@
 
 
 def kernel(
-    n, inside,
-    bank_row, lang_ids, seg_ids, lookback, frames, w_query, w_key, w_value, down, up,
+    n,
+    bank_row_any, lang_any, seg_any, look_any, frames, w_query, w_key, w_value, down, up,
     out,
+    bank_row, lang_ids, seg_ids, lookback,
     x, wq, wk, wv, d_mine, u_mine, d_bank, u_bank, d_send, u_send, q_two, acc, top, tot,
     local_sem, f_send, f_recv, t_send, t_recv, a_send, a_recv, dt_send, dt_recv,
 ):
@@ -38,13 +39,14 @@
         return pltpu.make_async_copy(src, dst, local_sem.at[i])
 
     own = local(frames, x.at[0, h], 0)
+    tables = [
+        local(bank_row_any, bank_row, 6), local(lang_any, lang_ids, 7),
+        local(seg_any, seg_ids, 8), local(look_any, lookback, 9)]
+    for c in tables:
+        c.start()
     own.start()
-    if inside:
-        bank_d = local(down, d_bank, 4)
-        bank_u = local(up, u_bank, 5)
-    else:
-        bank_d = local(down, d_mine, 4)
-        bank_u = local(up, u_mine, 5)
+    bank_d = local(down, d_bank, 4)
+    bank_u = local(up, u_bank, 5)
     bank_d.start()
     bank_u.start()
     weights = [local(w_query, wq, 1), local(w_key, wk, 2), local(w_value, wv, 3)]
@@ -53,10 +55,7 @@
 
     barrier = pltpu.get_barrier_semaphore()
     twin = {"head": 1 - h}
-    if inside:
-        steps = list(range(1, n))
-    else:
-        steps = [1, 2, 3, n - 3, n - 2, n - 1]
+    steps = range(1, n)
     pl.semaphore_signal(barrier, inc=1, device_id=twin, device_id_type=MESH)
     for k in steps:
         pl.semaphore_signal(barrier, inc=1, device_id={"seq": lax.rem(me + k, n)}, device_id_type=MESH)
@@ -73,6 +72,8 @@
             send_sem=t_send.at[d], recv_sem=t_recv.at[d], device_id=twin, device_id_type=MESH)
 
     twin_copy(0).start()
+    for c in tables:
+        c.wait()
 
     def adapter_copies(k):
         to = {"seq": lax.rem(me + k, n)}
@@ -94,20 +95,19 @@
                 src_ref=u_send.at[k - 1], dst_ref=u_mine.at[source], send_sem=a_send.at[1, k - 1],
                 recv_sem=a_recv.at[1, k - 1], device_id=twin, device_id_type=MESH))
 
-    if inside:
-        piece = d_send.shape[1]
-        first = pl.multiple_of(h * piece, piece)
-        bank_d.wait()
-        bank_u.wait()
-        for k in range(1, n):
-            row = bank_row[lang_ids[lax.rem(me + k, n)]]
-            d_send[k - 1] = d_bank[row, pl.ds(first, piece), :]
-            u_send[k - 1] = u_bank[row]
-            for c in adapter_copies(k):
-                c.start()
-        row = bank_row[lang_ids[me]]
-        d_mine[me, h] = d_bank[row, pl.ds(first, piece), :]
-        u_mine[me] = u_bank[row]
+    piece = d_send.shape[1]
+    first = pl.multiple_of(h * piece, piece)
+    bank_d.wait()
+    bank_u.wait()
+    for k in range(1, n):
+        row = bank_row[lang_ids[lax.rem(me + k, n)]]
+        d_send[k - 1] = d_bank[row, pl.ds(first, piece), :]
+        u_send[k - 1] = u_bank[row]
+        for c in adapter_copies(k):
+            c.start()
+    row = bank_row[lang_ids[me]]
+    d_mine[me, h] = d_bank[row, pl.ds(first, piece), :]
+    u_mine[me] = u_bank[row]
 
     for d in range(1, LOOK + 1):
         @pl.when(me + d < n)
@@ -131,18 +131,14 @@
         q_two[0, :, j * 128:(j + 1) * 128] = jnp.where(low, part, jnp.zeros_like(part))
         q_two[1, :, j * 128:(j + 1) * 128] = jnp.where(low, jnp.zeros_like(part), part)
 
-    if inside:
-        for k in range(1, n):
-            for c in adapter_arrivals(k):
-                c.wait_recv()
-        d_hand = pltpu.make_async_remote_copy(
-            src_ref=d_mine.at[:, h], dst_ref=d_mine.at[:, h], send_sem=dt_send, recv_sem=dt_recv,
-            device_id=twin, device_id_type=MESH)
-        d_hand.start()
-        d_hand.wait_recv()
-    else:
-        bank_d.wait()
-        bank_u.wait()
+    for k in range(1, n):
+        for c in adapter_arrivals(k):
+            c.wait_recv()
+    d_hand = pltpu.make_async_remote_copy(
+        src_ref=d_mine.at[:, h], dst_ref=d_mine.at[:, h], send_sem=dt_send, recv_sem=dt_recv,
+        device_id=twin, device_id_type=MESH)
+    d_hand.start()
+    d_hand.wait_recv()
 
     def hand_over(d):
         @pl.when(me >= d)
@@ -221,11 +217,131 @@
             @pl.when(me + d < n)
             def _():
                 frame_copy(d).wait_send()
-    if inside:
-        for k in range(1, n):
-            for c in adapter_copies(k):
-                c.wait_send()
-        d_hand.wait_send()
+    for k in range(1, n):
+        for c in adapter_copies(k):
+            c.wait_send()
+    d_hand.wait_send()
+
+
+def from_behind(block, axis, distance):
+    devices = range(lax.axis_size(axis))
+    route = [(i - distance, i) for i in devices if i - distance in devices]
+    return lax.ppermute(block, axis, route)
+
+
+def block_rules(seg_ids, lookback, position, distance, blocks_dev, block_len):
+    query_first = position * blocks_dev
+    key_first = (position - distance) * blocks_dev
+    counter = jnp.arange(blocks_dev, dtype=jnp.int32)
+    query_blocks = query_first + counter
+    key_blocks = key_first + counter
+    query_seg = lax.dynamic_slice_in_dim(seg_ids, query_first, blocks_dev)
+    query_reach = lax.dynamic_slice_in_dim(lookback, query_first, blocks_dev)
+    key_seg = lax.dynamic_slice_in_dim(seg_ids, jnp.maximum(key_first, 0), blocks_dev)
+    allowed = key_blocks[None, :] >= query_blocks[:, None] - query_reach[:, None]
+    allowed = allowed & (key_blocks[None, :] <= query_blocks[:, None])
+    allowed = allowed & (key_seg[None, :] == query_seg[:, None]) & (key_blocks[None, :] >= 0)
+    frames_dev = blocks_dev * block_len
+    expanded = jnp.broadcast_to(
+        allowed[:, None, :, None], (blocks_dev, block_len, blocks_dev, block_len)
+    )
+    return (jnp.any(allowed), expanded.reshape(frames_dev, frames_dev))
+
+
+def attend(carried, query_heads, pair, allowed):
+    run_max, run_sum, run_acc = carried
+    frames_dev = query_heads.shape[0]
+    heads_dev = query_heads.shape[1]
+    key_heads = pair[0].reshape(frames_dev, heads_dev, HD)
+    value_heads = pair[1].reshape(frames_dev, heads_dev, HD)
+    scores = jnp.einsum(
+        "qhe,khe->hqk", query_heads, key_heads, preferred_element_type=jnp.float32
+    ) * HD ** (-0.5)
+    masked = jnp.where(allowed[None], scores, NEG_LARGE)
+    new_max = jnp.maximum(run_max, jnp.max(masked, axis=2))
+    factor = jnp.exp(run_max - new_max)
+    weights = jnp.where(allowed[None], jnp.exp(masked - new_max[:, :, None]), 0.0)
+    new_sum = run_sum * factor + jnp.sum(weights, axis=2)
+    update = jnp.einsum(
+        "hqk,khe->hqe",
+        weights.astype(jnp.bfloat16),
+        value_heads,
+        preferred_element_type=jnp.float32,
+    )
+    return (new_max, new_sum, run_acc * factor[:, :, None] + update)
+
+
+def plain_body(
+    frames, w_query, w_key, w_value, down_bank, up_bank, bank_row, lang_ids, seg_ids, lookback
+):
+    seq_count = lax.axis_size("seq")
+    position = lax.axis_index("seq")
+    frames_dev = frames.shape[0]
+    blocks_dev = lang_ids.shape[0] // seq_count
+    block_len = frames_dev // blocks_dev
+    model_width = w_query.shape[0]
+    columns = w_query.shape[1]
+    heads_dev = columns // HD
+    rank_two = down_bank.shape[2]
+    rank_half = rank_two // 2
+    wanted = jnp.transpose(jnp.take(bank_row, lang_ids, axis=0).reshape(seq_count, blocks_dev))
+    picked = (wanted[:, :, None] == jnp.arange(down_bank.shape[0])).astype(jnp.bfloat16)
+    down_send = jnp.einsum("wbl,lrc->wbrc", picked, down_bank)
+    up_send = jnp.einsum("wbl,lrc->wbrc", picked, up_bank)
+    down_got, up_got = (
+        lax.all_to_all(down_send, "seq", split_axis=1, concat_axis=2, tiled=True),
+        lax.all_to_all(up_send, "seq", split_axis=1, concat_axis=2, tiled=True),
+    )
+    down_mine = down_got.reshape(blocks_dev, model_width, rank_two)
+    up_mine = up_got.reshape(blocks_dev, rank_two, columns)
+    gathered = lax.all_gather(frames, "head", axis=1, tiled=True)
+    queries = jnp.dot(gathered, w_query, preferred_element_type=jnp.float32).astype(jnp.bfloat16)
+    block_rows = gathered.reshape(blocks_dev, block_len, model_width)
+    lowrank = jnp.einsum(
+        "bfd,bdr->bfr", block_rows, down_mine, preferred_element_type=jnp.float32
+    ).astype(jnp.bfloat16)
+    key_extra = jnp.einsum(
+        "bfr,brc->bfc",
+        lowrank[:, :, :rank_half],
+        up_mine[:, :rank_half],
+        preferred_element_type=jnp.float32,
+    )
+    value_extra = jnp.einsum(
+        "bfr,brc->bfc",
+        lowrank[:, :, rank_half:],
+        up_mine[:, rank_half:],
+        preferred_element_type=jnp.float32,
+    )
+    own_keys = (
+        jnp.dot(gathered, w_key, preferred_element_type=jnp.float32)
+        + key_extra.reshape(frames_dev, columns)
+    ).astype(jnp.bfloat16)
+    own_values = (
+        jnp.dot(gathered, w_value, preferred_element_type=jnp.float32)
+        + value_extra.reshape(frames_dev, columns)
+    ).astype(jnp.bfloat16)
+    own_pair = jnp.stack([own_keys, own_values])
+    query_heads = queries.reshape(frames_dev, heads_dev, HD)
+    initial = (
+        jnp.full((heads_dev, frames_dev), NEG_LARGE, jnp.float32),
+        jnp.zeros((heads_dev, frames_dev), jnp.float32),
+        jnp.zeros((heads_dev, frames_dev, HD), jnp.float32),
+    )
+
+    def visit_tile(carried, pair, distance):
+        nonempty, allowed = block_rules(
+            seg_ids, lookback, position, distance, blocks_dev, block_len
+        )
+        return attend(carried, query_heads, pair, allowed)
+
+    carried = visit_tile(initial, own_pair, 0)
+    moving = own_pair
+    for distance in range(1, 4):
+        moving = from_behind(moving, "seq", 1)
+        carried = visit_tile(carried, moving, distance)
+    run_max, run_sum, run_acc = carried
+    context = (run_acc / run_sum[:, :, None]).astype(jnp.bfloat16)
+    return jnp.transpose(context, (1, 0, 2)).reshape(frames_dev, columns)
 
 
 def body(frames, w_query, w_key, w_value, down_bank, up_bank, bank_row, lang_ids, seg_ids, lookback):
@@ -234,29 +350,21 @@
     columns = w_query.shape[1]
     bank_rows, d_rows, rank_two = down_bank.shape
     u_rows = up_bank.shape[1]
-    inside = d_rows % 32 == 0 and u_rows % 16 == 0
+    if d_rows % 32 or u_rows % 16 or lang_ids.shape[0] != n:
+        return plain_body(
+            frames, w_query, w_key, w_value, down_bank, up_bank, bank_row, lang_ids, seg_ids, lookback)
     bf16, f32 = jnp.bfloat16, jnp.float32
-    if inside:
-        down, up = down_bank, up_bank
-        d_shape, u_shape = (n, 2, d_rows // 2, rank_two), (n, u_rows, columns)
-        banks = [down_bank.shape, up_bank.shape, (n - 1, d_rows // 2, rank_two), (n - 1, u_rows, columns)]
-    else:
-        wanted = jnp.take(bank_row, lang_ids, axis=0)
-        down = lax.all_to_all(jnp.take(down_bank, wanted, axis=0), "seq", split_axis=0, concat_axis=1, tiled=True)
-        up = lax.all_to_all(jnp.take(up_bank, wanted, axis=0), "seq", split_axis=0, concat_axis=1, tiled=True)
-        down, up = down.reshape(d_rows * n, rank_two), up.reshape(u_rows * n, columns)
-        d_shape, u_shape = down.shape, up.shape
-        banks = [(16, 128)] * 4
-    steps = n - 1 if inside else 1
-    smem = pl.BlockSpec(memory_space=pltpu.SMEM)
-    anywhere = pl.BlockSpec(memory_space=pl.ANY)
+    d_shape, u_shape = (n, 2, d_rows // 2, rank_two), (n, u_rows, columns)
+    banks = [down_bank.shape, up_bank.shape, (n - 1, d_rows // 2, rank_two), (n - 1, u_rows, columns)]
+    hbm = pl.BlockSpec(memory_space=pltpu.HBM)
     dma = pltpu.SemaphoreType.DMA
     return pl.pallas_call(
-        functools.partial(kernel, n, inside),
+        functools.partial(kernel, n),
         out_shape=jax.ShapeDtypeStruct((rows, columns), bf16),
-        in_specs=[smem] * 4 + [anywhere] * 6,
+        in_specs=[hbm] * 10,
         out_specs=pl.BlockSpec(memory_space=pltpu.VMEM),
         scratch_shapes=[
+            *[pltpu.SMEM(t.shape, jnp.int32) for t in (bank_row, lang_ids, seg_ids, lookback)],
             pltpu.VMEM((LOOK + 1, 2, rows, half), bf16),
             *[pltpu.VMEM(w_query.shape, bf16)] * 3,
             pltpu.VMEM(d_shape, bf16),
@@ -265,13 +373,13 @@
             pltpu.VMEM((2, rows, columns), bf16),
             pltpu.VMEM((rows, columns), f32),
             *[pltpu.VMEM((columns // HD, rows, 128), f32)] * 2,
-            dma((6,)), dma((LOOK,)), dma((LOOK,)), dma((LOOK + 1,)), dma((LOOK + 1,)),
-            dma((2, steps)), dma((2, steps)), dma, dma,
+            dma((10,)), dma((LOOK,)), dma((LOOK,)), dma((LOOK + 1,)), dma((LOOK + 1,)),
+            dma((2, n - 1)), dma((2, n - 1)), dma, dma,
         ],
         compiler_params=pltpu.CompilerParams(
-            collective_id=0, has_side_effects=True, vmem_limit_bytes=50 * 2 ** 20),
+            collective_id=0, has_side_effects=True, vmem_limit_bytes=60 * 2 ** 20),
         cost_estimate=pl.CostEstimate(flops=6 * 10 ** 9, bytes_accessed=8 * 2 ** 20, transcendentals=2 ** 21),
-    )(bank_row, lang_ids, seg_ids, lookback, frames, w_query, w_key, w_value, down, up)
+    )(bank_row, lang_ids, seg_ids, lookback, frames, w_query, w_key, w_value, down_bank, up_bank)
 
 
 def solution(mesh):

time: 53.6 us -> 45.1 us (0.84)
  local copies, waits for them, and re-layouts: 9.8 us -> 1.67 us
    unnamed x21 -> x1, local copies, waits for them, and re-layouts: 9.8 us -> 1.67 us
where the time goes in v2:
time: 45.1 us; the launch traced here: 44.9 us
  Pallas kernels  43.2 us (96%)
  local copies, waits for them, and re-layouts  1.67 us (4%)
    pallas_call x1, Pallas kernels, body(): pl.pallas_call(functools.partial(kernel, n), out_shape=jax.ShapeDtypeStru...  43.2 us
    unnamed x1, local copies, waits for them, and re-layouts  1.67 us

profile of v2, /device:TPU:18, one launch (start us, length us, event | category | flops | bytes accessed | tf_op | source)
XLA Modules:
  0.0 44.9 jit_solution(16407457332338476026)
XLA Ops:
  0.0 43.2 %shard_map.100 = bf16[256,512]{1,0:T(8,128)(2,1)} custom-call(s32[8]{0:T(128)} %bank_row_any.1, s32[8]{0:T(128)} %lang_any.1, s32[8]{0:T(128)} %seg_any.1, s32[8]{0:T(128)} %look_any.1, bf16[256,512]{1,0:T(8,128)(2,1)} %frames.1, bf16[1024,512]{1,0:T(8,128)(2,1)} %w_query.1, bf16[1024,512]{1,0:T(8,128)(2,1)} %w_key.1, bf16[1024,512]{1,0:T(8,128)(2,1)} %w_value.1, ...), custom_call_target="tpu_custom_call" | custom-call | flops 6000000000 | bytes 8388608 | tf_op jit(solution)/shard_map/pallas_call | solution.py:361
  43.2 1.7 %copy.12 = bf16[256,512]{1,0:T(8,128)(2,1)} copy(bf16[256,512]{1,0:T(8,128)(2,1)} %shard_map.100) | data formatting | bytes 524288

commit v3 on v2

--- a/solution.py
+++ b/solution.py
@@ -9,6 +9,7 @@
 
 HD = 64
 LOOK = 3
+CHUNKS = 2
 NEG_LARGE = -1e30
 MESH = pl.DeviceIdType.MESH
 
@@ -61,15 +62,30 @@
         pl.semaphore_signal(barrier, inc=1, device_id={"seq": lax.rem(me + k, n)}, device_id_type=MESH)
     pl.semaphore_wait(barrier, len(steps) + 1)
 
-    def frame_copy(d):
+    even = lax.rem(me, 2) == 0
+    size = rows // CHUNKS
+
+    def frame_copy(kind, c, slot, source, to):
+        part = pl.ds(c * size, size)
         return pltpu.make_async_remote_copy(
-            src_ref=frames, dst_ref=x.at[d, h], send_sem=f_send.at[d - 1], recv_sem=f_recv.at[d - 1],
-            device_id={"seq": lax.rem(me + d, n)}, device_id_type=MESH)
-
-    def twin_copy(d):
+            src_ref=frames.at[part] if source == 0 else x.at[source, h, part],
+            dst_ref=x.at[slot, h, part], send_sem=f_send.at[kind, c], recv_sem=f_recv.at[slot - 1, c],
+            device_id={"seq": lax.rem(me + to + n, n)}, device_id_type=MESH)
+
+    def twin_copy(d, c=0):
+        part = pl.ds(c * size, size) if d else pl.ds(0, rows)
         return pltpu.make_async_remote_copy(
-            src_ref=frames if d == 0 else x.at[d, h], dst_ref=x.at[d, h],
-            send_sem=t_send.at[d], recv_sem=t_recv.at[d], device_id=twin, device_id_type=MESH)
+            src_ref=x.at[d, h, part] if d else frames, dst_ref=x.at[d, h, part],
+            send_sem=t_send.at[d, c], recv_sem=t_recv.at[d, c], device_id=twin, device_id_type=MESH)
+
+    for c in range(CHUNKS):
+        @pl.when(me + 2 < n)
+        def _():
+            frame_copy(0, c, 2, 0, 2).start()
+
+        @pl.when(even)
+        def _():
+            frame_copy(1, c, 1, 0, 1).start()
 
     twin_copy(0).start()
     for c in tables:
@@ -109,11 +125,6 @@
     d_mine[me, h] = d_bank[row, pl.ds(first, piece), :]
     u_mine[me] = u_bank[row]
 
-    for d in range(1, LOOK + 1):
-        @pl.when(me + d < n)
-        def _():
-            frame_copy(d).start()
-
     lane = lax.broadcasted_iota(jnp.int32, (rows, 128), 1)
     low = lane < HD
 
@@ -131,6 +142,40 @@
         q_two[0, :, j * 128:(j + 1) * 128] = jnp.where(low, part, jnp.zeros_like(part))
         q_two[1, :, j * 128:(j + 1) * 128] = jnp.where(low, jnp.zeros_like(part), part)
 
+    def hand_over(d):
+        for c in range(CHUNKS):
+            @pl.when(me >= d)
+            def _():
+                frame_copy(0, c, d, 0, 2).wait_recv()
+
+            if d == 2:
+                @pl.when(even & (me >= 2))
+                def _():
+                    frame_copy(2, c, 3, 2, 1).start()
+
+                @pl.when((~even) & (me >= 3))
+                def _():
+                    frame_copy(2, c, 1, 2, -1).start()
+            if d == 1:
+                @pl.when(even & (me >= 2) & (me + 2 < n))
+                def _():
+                    frame_copy(3, c, 3, 1, 2).start()
+
+            @pl.when(me >= d)
+            def _():
+                twin_copy(d, c).start()
+
+        @pl.when(me < d)
+        def _():
+            x[d] = jnp.zeros(x.shape[1:], x.dtype)
+
+    def arrived(d):
+        for c in range(CHUNKS):
+            @pl.when(me >= d)
+            def _():
+                twin_copy(d, c).wait_recv()
+
+    hand_over(2)
     for k in range(1, n):
         for c in adapter_arrivals(k):
             c.wait_recv()
@@ -139,21 +184,6 @@
         device_id=twin, device_id_type=MESH)
     d_hand.start()
     d_hand.wait_recv()
-
-    def hand_over(d):
-        @pl.when(me >= d)
-        def _():
-            frame_copy(d).wait_recv()
-            twin_copy(d).start()
-
-        @pl.when(me < d)
-        def _():
-            x[d] = jnp.zeros(x.shape[1:], x.dtype)
-
-    def arrived(d):
-        @pl.when(me >= d)
-        def _():
-            twin_copy(d).wait_recv()
 
     def keys_values(d):
         flat_d = d_mine[...].reshape(2 * half, 128)
@@ -201,22 +231,37 @@
                 acc[:, cols] = new
 
     attend(0)
-    for d in range(1, LOOK + 1):
-        hand_over(d)
-        arrived(d)
-        attend(d)
-
-    for d in range(LOOK + 1):
-        if d == 0:
-            twin_copy(0).wait_send()
-        else:
+    hand_over(1)
+    arrived(2)
+    attend(2)
+    arrived(1)
+    attend(1)
+    hand_over(3)
+    arrived(3)
+    attend(3)
+
+    twin_copy(0).wait_send()
+    for c in range(CHUNKS):
+        for d in range(1, LOOK + 1):
             @pl.when(me >= d)
             def _():
-                twin_copy(d).wait_send()
-
-            @pl.when(me + d < n)
-            def _():
-                frame_copy(d).wait_send()
+                twin_copy(d, c).wait_send()
+
+        @pl.when(me + 2 < n)
+        def _():
+            frame_copy(0, c, 2, 0, 2).wait_send()
+
+        @pl.when(even)
+        def _():
+            frame_copy(1, c, 1, 0, 1).wait_send()
+
+        @pl.when(me >= 2)
+        def _():
+            frame_copy(2, c, 3, 2, 1).wait_send()
+
+        @pl.when(even & (me >= 2) & (me + 2 < n))
+        def _():
+            frame_copy(3, c, 3, 1, 2).wait_send()
     for k in range(1, n):
         for c in adapter_copies(k):
             c.wait_send()
@@ -350,7 +395,7 @@
     columns = w_query.shape[1]
     bank_rows, d_rows, rank_two = down_bank.shape
     u_rows = up_bank.shape[1]
-    if d_rows % 32 or u_rows % 16 or lang_ids.shape[0] != n:
+    if n % 2 or d_rows % 32 or u_rows % 16 or lang_ids.shape[0] != n:
         return plain_body(
             frames, w_query, w_key, w_value, down_bank, up_bank, bank_row, lang_ids, seg_ids, lookback)
     bf16, f32 = jnp.bfloat16, jnp.float32
@@ -373,7 +418,7 @@
             pltpu.VMEM((2, rows, columns), bf16),
             pltpu.VMEM((rows, columns), f32),
             *[pltpu.VMEM((columns // HD, rows, 128), f32)] * 2,
-            dma((10,)), dma((LOOK,)), dma((LOOK,)), dma((LOOK + 1,)), dma((LOOK + 1,)),
+            dma((10,)), dma((4, CHUNKS)), dma((LOOK, CHUNKS)), *[dma((LOOK + 1, CHUNKS))] * 2,
             dma((2, n - 1)), dma((2, n - 1)), dma, dma,
         ],
         compiler_params=pltpu.CompilerParams(

time: 45.1 us -> 41.5 us (0.920)
  the two profiles are of different devices: /device:TPU:18 before, /device:TPU:24 now
where the time goes in v3:
time: 41.5 us; the launch traced here: 41.1 us
  Pallas kernels  39.4 us (95%)
  local copies, waits for them, and re-layouts  1.67 us (4%)
    pallas_call x1, Pallas kernels, body(): pl.pallas_call(functools.partial(kernel, n), out_shape=jax.ShapeDtypeStru...  39.4 us
    unnamed x1, local copies, waits for them, and re-layouts  1.67 us

profile of v3, /device:TPU:24, one launch (start us, length us, event | category | flops | bytes accessed | tf_op | source)
XLA Modules:
  0.0 41.1 jit_solution(15026262490461058770)
XLA Ops:
  0.0 39.4 %shard_map.100 = bf16[256,512]{1,0:T(8,128)(2,1)} custom-call(s32[8]{0:T(128)} %bank_row_any.1, s32[8]{0:T(128)} %lang_any.1, s32[8]{0:T(128)} %seg_any.1, s32[8]{0:T(128)} %look_any.1, bf16[256,512]{1,0:T(8,128)(2,1)} %frames.1, bf16[1024,512]{1,0:T(8,128)(2,1)} %w_query.1, bf16[1024,512]{1,0:T(8,128)(2,1)} %w_key.1, bf16[1024,512]{1,0:T(8,128)(2,1)} %w_value.1, ...), custom_call_target="tpu_custom_call" | custom-call | flops 6000000000 | bytes 8388608 | tf_op jit(solution)/shard_map/pallas_call | solution.py:406
  39.4 1.7 %copy.12 = bf16[256,512]{1,0:T(8,128)(2,1)} copy(bf16[256,512]{1,0:T(8,128)(2,1)} %shard_map.100) | data formatting | bytes 524288

commit v4 on v3

--- a/solution.py
+++ b/solution.py
@@ -202,30 +202,34 @@
             bias = jnp.where(allowed, 0.0, NEG_LARGE).astype(jnp.float32)
         for j in range(pairs):
             cols = slice(j * 128, (j + 1) * 128)
-            outs, factors = [], []
+            outs, factors, totals = [], [], []
             for e in range(2):
                 head = 2 * j + e
                 s = dot_t(q_two[e, :, cols], key[:, cols])
-                if d == 0:
-                    m = jnp.max(s, axis=1, keepdims=True)
-                    w = jnp.exp(s - m)
-                    total = jnp.sum(w, axis=1, keepdims=True)
+                if d > 0:
+                    s = s + bias
+                m = jnp.broadcast_to(jnp.max(s, axis=1, keepdims=True), (rows, 128))
+                if d > 0:
+                    before = top[head]
+                    m = jnp.maximum(before, m)
+                    factor = jnp.exp(before - m)
+                    factors.append(factor)
+                parts = [jnp.exp(s[:, i:i + 128] - m) for i in range(0, rows, 128)]
+                total = sum(parts[1:], parts[0])
+                if d > 0:
+                    total = total + tot[head] * factor
+                if d == LOOK:
+                    totals.append(jnp.sum(total, axis=1, keepdims=True))
                 else:
-                    s = s + bias
-                    before = top[head][:, :1]
-                    m = jnp.maximum(before, jnp.max(s, axis=1, keepdims=True))
-                    w = jnp.exp(s - m)
-                    factor = jnp.exp(before - m)
-                    total = tot[head][:, :1] * factor + jnp.sum(w, axis=1, keepdims=True)
-                    factors.append(factor)
-                top[head] = jnp.broadcast_to(m, (rows, 128))
-                tot[head] = jnp.broadcast_to(total, (rows, 128))
-                outs.append(dot(w.astype(jnp.bfloat16), value[:, cols]))
+                    top[head] = m
+                    tot[head] = total
+                w = jnp.concatenate([p.astype(jnp.bfloat16) for p in parts], axis=1)
+                outs.append(dot(w, value[:, cols]))
             new = jnp.where(low, outs[0], outs[1])
             if d > 0:
                 new = new + acc[:, cols] * jnp.where(low, factors[0], factors[1])
             if d == LOOK:
-                new = new / jnp.where(low, tot[2 * j], tot[2 * j + 1])
+                new = new / jnp.where(low, totals[0], totals[1])
                 out[:, cols] = new.astype(out.dtype)
             else:
                 acc[:, cols] = new

time: 41.5 us -> 29.8 us (0.72)
  Pallas kernels: 39.4 us -> 27.8 us
    pallas_call x1, Pallas kernels: 39.4 us -> 27.8 us  [body(): pl.pallas_call(functools.partial(kernel, n), out_shape=jax.ShapeDtypeStru...]
where the time goes in v4:
time: 29.8 us; the launch traced here: 29.4 us
  Pallas kernels  27.8 us (93%)
  local copies, waits for them, and re-layouts  1.67 us (6%)
    pallas_call x1, Pallas kernels, body(): pl.pallas_call(functools.partial(kernel, n), out_shape=jax.ShapeDtypeStru...  27.8 us
    unnamed x1, local copies, waits for them, and re-layouts  1.67 us

profile of v4, /device:TPU:24, one launch (start us, length us, event | category | flops | bytes accessed | tf_op | source)
XLA Modules:
  0.0 29.4 jit_solution(10534807036904915079)
XLA Ops:
  0.0 27.8 %shard_map.100 = bf16[256,512]{1,0:T(8,128)(2,1)} custom-call(s32[8]{0:T(128)} %bank_row_any.1, s32[8]{0:T(128)} %lang_any.1, s32[8]{0:T(128)} %seg_any.1, s32[8]{0:T(128)} %look_any.1, bf16[256,512]{1,0:T(8,128)(2,1)} %frames.1, bf16[1024,512]{1,0:T(8,128)(2,1)} %w_query.1, bf16[1024,512]{1,0:T(8,128)(2,1)} %w_key.1, bf16[1024,512]{1,0:T(8,128)(2,1)} %w_value.1, ...), custom_call_target="tpu_custom_call" | custom-call | flops 6000000000 | bytes 8388608 | tf_op jit(solution)/shard_map/pallas_call | solution.py:410
  27.8 1.7 %copy.12 = bf16[256,512]{1,0:T(8,128)(2,1)} copy(bf16[256,512]{1,0:T(8,128)(2,1)} %shard_map.100) | data formatting | bytes 524288

commit v5 on v4

--- a/solution.py
+++ b/solution.py
@@ -9,7 +9,7 @@
 
 HD = 64
 LOOK = 3
-CHUNKS = 2
+CHUNKS = 4
 NEG_LARGE = -1e30
 MESH = pl.DeviceIdType.MESH
 
@@ -142,6 +142,8 @@
         q_two[0, :, j * 128:(j + 1) * 128] = jnp.where(low, part, jnp.zeros_like(part))
         q_two[1, :, j * 128:(j + 1) * 128] = jnp.where(low, jnp.zeros_like(part), part)
 
+    own_base = (project(0, wk), project(0, wv))
+
     def hand_over(d):
         for c in range(CHUNKS):
             @pl.when(me >= d)
@@ -190,8 +192,9 @@
         flat_u = u_mine[...].reshape(128, columns)
         low_rank = (dot(x[d, 0], flat_d[:half]) + dot(x[d, 1], flat_d[half:])).astype(jnp.bfloat16)
         none = jnp.zeros_like(low_rank)
-        key = (project(d, wk) + dot(jnp.where(low, low_rank, none), flat_u)).astype(jnp.bfloat16)
-        value = (project(d, wv) + dot(jnp.where(low, none, low_rank), flat_u)).astype(jnp.bfloat16)
+        base = (project(d, wk), project(d, wv)) if d else own_base
+        key = (base[0] + dot(jnp.where(low, low_rank, none), flat_u)).astype(jnp.bfloat16)
+        value = (base[1] + dot(jnp.where(low, none, low_rank), flat_u)).astype(jnp.bfloat16)
         return key, value
 
     def attend(d):

time: 29.8 us -> 29.7 us (level)
  no operation moved by 1% of the time
where the time goes in v5:
time: 29.7 us; the launch traced here: 29.3 us
  Pallas kernels  27.6 us (93%)
  local copies, waits for them, and re-layouts  1.67 us (6%)
    pallas_call x1, Pallas kernels, body(): pl.pallas_call(functools.partial(kernel, n), out_shape=jax.ShapeDtypeStru...  27.6 us
    unnamed x1, local copies, waits for them, and re-layouts  1.67 us

profile of v5, /device:TPU:24, one launch (start us, length us, event | category | flops | bytes accessed | tf_op | source)
XLA Modules:
  0.0 29.3 jit_solution(11773762743104656120)
XLA Ops:
  0.0 27.6 %shard_map.100 = bf16[256,512]{1,0:T(8,128)(2,1)} custom-call(s32[8]{0:T(128)} %bank_row_any.1, s32[8]{0:T(128)} %lang_any.1, s32[8]{0:T(128)} %seg_any.1, s32[8]{0:T(128)} %look_any.1, bf16[256,512]{1,0:T(8,128)(2,1)} %frames.1, bf16[1024,512]{1,0:T(8,128)(2,1)} %w_query.1, bf16[1024,512]{1,0:T(8,128)(2,1)} %w_key.1, bf16[1024,512]{1,0:T(8,128)(2,1)} %w_value.1, ...), custom_call_target="tpu_custom_call" | custom-call | flops 6000000000 | bytes 8388608 | tf_op jit(solution)/shard_map/pallas_call | solution.py:413
  27.6 1.7 %copy.12 = bf16[256,512]{1,0:T(8,128)(2,1)} copy(bf16[256,512]{1,0:T(8,128)(2,1)} %shard_map.100) | data formatting | bytes 524288
